TPU v7x, 256 devices: a whole 4x4x8 slice. The times are simulated.
256 devices in a mesh: ia: 8 (over z_lo, x), ja: 8 (over z_hi, core), ka: 4 (over y).
Axes of the slice: x: 4, y: 4, z: 8 (z_hi: 4, z_lo: 2; z = z_hi * 2 + z_lo), core: 2. Of those that a mesh axis runs over, the one named last changes fastest.
Arguments:
- tensor: bfloat16 [16384, 128, 512], P('ia', 'ja', 'ka'), may hold values from 0 to 8
- factor_b: bfloat16 [128, 64], P(('ja', 'ka')), may hold values from 0.049804688 to 1
- factor_c: bfloat16 [512, 64], P('ka'), may hold values from 0.049804688 to 1
- factor_a: float32 [16384, 64], P(('ia', 'ja', 'ka')), may hold values from 0 to 1
- restart: int32 [12], replicated, may hold values 0 or 1
Outputs:
- updated: float32 [16384, 64], P(('ia', 'ja', 'ka'))
- gram_a: float32 [64, 64], replicated
All inputs are finite; a program needn't handle non-finite values.
Results may differ from a plain program's by a relative error of at most 0.0003.
Values may be sent and summed in bfloat16 or wider, within the bound.
A program may use at most 64 MiB of HBM per device.

v0:
```python
import jax
import jax.numpy as jnp
from jax import lax
from jax.sharding import PartitionSpec as P

ITERS = 12


def shards(tensor, factor_b, factor_c, factor_a, restart):
    rows, cols, depth = tensor.shape
    rank = factor_c.shape[1]
    b_block = lax.all_gather(factor_b, "ka", axis=0, tiled=True)
    b_wide = b_block.astype(jnp.float32)
    own_rows = factor_a.shape[0]
    partial_value = jnp.dot(
        tensor.reshape(rows * cols, depth), factor_c, preferred_element_type=jnp.float32
    ).reshape(rows, cols, rank)
    total = lax.psum(jnp.sum(partial_value * b_wide[None, :, :], axis=1), ("ja", "ka"))
    where = lax.axis_index(("ja", "ka"))
    mttkrp = lax.dynamic_slice_in_dim(total, where * own_rows, own_rows, 0)
    local_b = jnp.dot(factor_b.T, factor_b, preferred_element_type=jnp.float32)
    local_c = jnp.dot(factor_c.T, factor_c, preferred_element_type=jnp.float32)
    gram_b = lax.psum(local_b, ("ja", "ka"))
    gram_c = lax.psum(local_c, "ka")
    gram = gram_b * gram_c
    lip = jnp.sqrt(jnp.sum(gram * gram))

    def one_step(step, carry):
        current, look, tval = carry
        flag = restart[step].astype(jnp.float32)
        look = flag * current + (1.0 - flag) * look
        tval = flag + (1.0 - flag) * tval
        grad = jnp.dot(look, gram, precision=lax.Precision.HIGHEST) - mttkrp
        nxt = jnp.maximum(look - grad / lip, 0.0)
        t_next = (1.0 + jnp.sqrt(1.0 + 4.0 * tval * tval)) / 2.0
        look = nxt + (tval - 1.0) / t_next * (nxt - current)
        return (nxt, look, t_next)

    current, look, tval = lax.fori_loop(0, ITERS, one_step, (factor_a, factor_a, jnp.float32(1.0)))
    local_a = jnp.dot(current.T, current, precision=lax.Precision.HIGHEST)
    gram_a = lax.psum(local_a, ("ia", "ja", "ka"))
    return (current, gram_a)


def solution(mesh):
    return jax.shard_map(
        shards,
        mesh=mesh,
        in_specs=(
            P("ia", "ja", "ka"),
            P(("ja", "ka"), None),
            P("ka", None),
            P(("ia", "ja", "ka"), None),
            P(),
        ),
        out_specs=(P(("ia", "ja", "ka"), None), P()),
        check_vma=False,
    )
```

profile of v0, /device:TPU:1, one launch (start us, length us, event | category | flops | bytes accessed | tf_op | source)
XLA Modules:
  0.0 421.5 jit_solution(16415912972680896458)
XLA Ops:
  7.2 0.0 copy-start
  7.2 0.0 all-reduce.2.cloned.1.call-start
  7.2 0.8 copy.31
  8.0 9.0 %all-gather = bf16[4,4,64]{2,1,0:T(4,128)(2,1)S(1)} all-gather(bf16[1,4,64]{2,1,0:T(4,128)(2,1)} %bitcast.19), channel_id=1, replica_groups=mesh['ia'=8,'ja'=8,'ka'=4] {'ka'}, dimensions={0}, use_global_device_ids=true | all-gather | bytes 2560 | tf_op jit(solution)/shard_map/all_gather | solution.py:12
  17.0 0.0 copy-done
  17.0 0.0 copy-start.2
  17.0 0.0 copy-start.3
  17.0 9.6 %multiply_reduce_fusion = f32[2048,64]{0,1:T(8,128)} fusion(bf16[2048,16,128]{2,1,0:T(8,128)(2,1)} %param.7, f32[16,64]{1,0:T(8,128)S(1)} %convert, bf16[128,64]{0,1:T(8,128)(2,1)S(1)} %copy-done), kind=kOutput, calls=%fused_computation.12 | convolution fusion | flops 540934144 | bytes 8933376 | tf_op jit(solution)/shard_map/dot_general | solution.py:15
  26.7 0.0 all-reduce.2.cloned.1.call-update
  26.7 0.0 copy-done.2
  26.7 0.2 fusion.13
  26.9 137.3 %psum.28 = f32[64,64]{1,0:T(8,128)S(1)} all-reduce(f32[64,64]{1,0:T(8,128)S(1)} %fusion.13), channel_id=1, replica_groups=mesh['ia'=8,'ja'=8,'ka'=4] {'ja','ka'}, use_global_device_ids=true, to_apply=%region_0.0 | all-reduce | flops 4096 | bytes 32768 | tf_op jit(solution)/shard_map/psum | solution.py:23
  164.2 0.1 fusion.14
  164.3 11.4 %psum.29 = f32[64,64]{1,0:T(8,128)S(1)} all-reduce(f32[64,64]{1,0:T(8,128)S(1)} %fusion.14), channel_id=1, replica_groups=mesh['ia'=8,'ja'=8,'ka'=4] {'ka'}, use_global_device_ids=true, to_apply=%region_1.0 | all-reduce | flops 4096 | bytes 32768 | tf_op jit(solution)/shard_map/psum | solution.py:24
  175.7 0.6 multiply_reduce_fusion.1
  177.0 135.3 %all-reduce.2.cloned.1.call-done = f32[2048,64]{0,1:T(8,128)} async-done(((f32[2048,64]{0,1:T(8,128)}), f32[2048,64]{0,1:T(8,128)}) %all-reduce.2.cloned.1.call-update) | async-done | bytes 524304 | tf_op jit(solution)/shard_map/psum | solution.py:18
  312.2 0.8 constant_dynamic-slice_fusion
  313.1 0.1 copy.9
  313.1 0.0 copy-done.3
  313.2 20.1 %while.19 = (s32[]{:T(128)}, f32[64,64]{1,0:T(8,128)S(1)}, f32[64,64]{1,0:T(8,128)S(1)}, f32[]{:T(128)}, s32[12]{0:T(128)S(1)}, /*index=5*/f32[64,64]{1,0:T(8,12...) while((s32[]{:T(128)}, f32[64,64]{1,0:T(8,128)S(1)}, ...), condition=%wide.region_6.0_spmd, body=%wide.region_5.0_spmd.sunk | while | flops 3198989 | bytes 164129 | solution.py:39
  313.2 0.7 dynamic_slice.16
  314.7 0.2 multiply_add_fusion.2
  314.9 0.7 dynamic_slice.16
  316.3 0.2 multiply_add_fusion.2
  316.5 0.7 dynamic_slice.16
  318.0 0.2 multiply_add_fusion.2
  318.2 0.7 dynamic_slice.16
  319.7 0.2 multiply_add_fusion.2
  319.9 0.7 dynamic_slice.16
  321.4 0.2 multiply_add_fusion.2
  321.6 0.7 dynamic_slice.16
  323.0 0.2 multiply_add_fusion.2
  323.2 0.7 dynamic_slice.16
  324.7 0.2 multiply_add_fusion.2
  324.9 0.7 dynamic_slice.16
  326.4 0.2 multiply_add_fusion.2
  326.6 0.7 dynamic_slice.16
  328.1 0.2 multiply_add_fusion.2
  328.3 0.7 dynamic_slice.16
  329.7 0.2 multiply_add_fusion.2
  329.9 0.7 dynamic_slice.16
  331.4 0.2 multiply_add_fusion.2
  331.6 0.7 dynamic_slice.16
  333.1 0.2 multiply_add_fusion.2
  333.3 0.0 copy-start.1
  333.3 0.2 fusion.15
  333.5 81.1 %psum.31 = f32[64,64]{1,0:T(8,128)} all-reduce(f32[64,64]{1,0:T(8,128)S(1)} %fusion.15), channel_id=1, replica_groups=mesh['ia'=8,'ja'=8,'ka'=4] {'ia','ja','ka'}, use_global_device_ids=true, to_apply=%region_7.0 | all-reduce | flops 4096 | bytes 32768 | tf_op jit(solution)/shard_map/psum | solution.py:41
  414.7 0.0 copy-done.1
  (26 shorter events, 0.1 us)
Async XLA Ops:
  7.2 9.9 %copy-start = (bf16[128,64]{0,1:T(8,128)(2,1)S(1)}, bf16[128,64]{0,1:T(8,128)(2,1)}, u32[]{:S(2)}) copy-start(bf16[128,64]{0,1:T(8,128)(2,1)} %param.9) | copy-start | bytes 49156
  7.2 305.1 %all-reduce.2.cloned.1.call-start = ((), (), s32[]{:S(2)}) async-start(), calls=%async_computation | async-start | bytes 1048576 | tf_op jit(solution)/shard_map/psum | solution.py:18
  17.0 9.7 %copy-start.2 = (bf16[4,64]{1,0:T(4,128)(2,1)S(1)}, bf16[4,64]{1,0:T(4,128)(2,1)}, u32[]{:S(2)}) copy-start(bf16[4,64]{1,0:T(4,128)(2,1)} %param.8) | copy-start | bytes 1540
  17.0 296.1 %copy-start.3 = (s32[12]{0:T(128)S(1)}, s32[12]{0:T(128)}, u32[]{:S(2)}) copy-start(s32[12]{0:T(128)} %param.11) | copy-start | bytes 148
  333.3 81.4 %copy-start.1 = (f32[64,64]{1,0:T(8,128)}, f32[64,64]{1,0:T(8,128)S(1)}, u32[]{:S(2)}) copy-start(f32[64,64]{1,0:T(8,128)S(1)} %get-tuple-element.198) | copy-start | bytes 49156
Sparse Core Ops, SparseCore 0:
  26.8 285.3 all-reduce.1
where the time goes:
time: 422 us
  blocking collectives  239 us (57%)
  waiting for transfers between devices  135 us (32%)
  between operations  14.8 us (4%)
  matrix products  12.3 us (3%)
  loops' own time  9.95 us (2%)
  local copies, waits for them, and re-layouts  9.79 us (2%)
    psum x1, blocking collectives, shards(): gram_b = lax.psum(local_b, ('ja', 'ka'))  137 us
    psum x1, waiting for transfers between devices, shards(): lax.psum(jnp.sum(partial_value * b_wide[None, :, :], axis=1), ('ja', 'ka'))  135 us
    psum x1, blocking collectives, shards(): gram_a = lax.psum(local_a, ('ia', 'ja', 'ka'))  81.1 us
    psum x1, blocking collectives, shards(): gram_c = lax.psum(local_c, 'ka')  11.4 us
    another operation x1, loops' own time, shards(): lax.fori_loop(0, ITERS, one_step, (factor_a, factor_a, jnp.float32(1.0)))  9.95 us
    dot_general x1, matrix products, shards(): jnp.dot(tensor.reshape(rows * cols, depth), factor_c, preferred_element_t...  9.65 us
    all_gather x1, blocking collectives, shards(): b_block = lax.all_gather(factor_b, 'ka', axis=0, tiled=True)  9.02 us
  transfers between devices with their start and end apart: 1, of which 1 were waited for; matrix products, arithmetic and copies ran while one was open for 0% of the time, Pallas kernels for 0%

commit v1 on v0

v1 whole, which is shorter than its diff:
```python
import functools

import jax
import jax.numpy as jnp
from jax import lax
from jax.experimental import pallas as pl
from jax.experimental.pallas import tpu as pltpu
from jax.sharding import PartitionSpec as P

ITERS = 12
MESH = pl.DeviceIdType.MESH
BLOCKS = 32
HALF = 32


def far_first(n):
    return 2 + n - (n // 2) * (2 * n - 1)


def add_rows(stack, row):
    for bit in (1, 2, 4):
        keep = (row & bit) == 0
        stack = [
            jnp.where(keep, u, v) + pltpu.roll(jnp.where(keep, v, u), 8 - bit, 0)
            for u, v in zip(stack[0::2], stack[1::2])
        ]
    return stack[0]


def split(value):
    high = value.astype(jnp.bfloat16)
    return high, (value - high.astype(jnp.float32)).astype(jnp.bfloat16)


def kernel(
    t_hbm, b_hbm, ct_hbm, a_hbm, restart_hbm, up_ref, gram_ref,
    t_ref, prod, b_in, ct_in, a_in, flags,
    b_slots, b_block, b_all, ct_all, weight_c,
    give, got, mine, out_rs, in_rs, weight_g, coef,
    gram_out, gram_z, gram_half, gram_xy,
    t_sem, in_sem, b_s, b_r, c_s, c_r, ball_s, ball_r,
    x_s, x_r, rs_s, rs_r, z_s, z_r, xy_s, xy_r,
):
    f32, bf16 = jnp.float32, jnp.bfloat16
    ia, ja, y = lax.axis_index("ia"), lax.axis_index("ja"), lax.axis_index("ka")
    z_lo, x, z_hi, core = ia // 4, ia % 4, ja // 2, ja % 2
    z = z_hi * 2 + z_lo

    def device(z, x, y, core):
        return ((z % 2) * 4 + x, (z // 2) * 2 + core, y)

    def remote(src, dst, send, recv, to):
        return pltpu.make_async_remote_copy(
            src_ref=src, dst_ref=dst, send_sem=send, recv_sem=recv, device_id=to, device_id_type=MESH
        )

    loads = [
        pltpu.make_async_copy(b_hbm, b_in, in_sem.at[0]),
        pltpu.make_async_copy(ct_hbm, ct_in, in_sem.at[1]),
        pltpu.make_async_copy(a_hbm, a_in, in_sem.at[2]),
        pltpu.make_async_copy(restart_hbm, flags, in_sem.at[3]),
    ]
    for load in loads:
        load.start()

    def tensor_load(n):
        return pltpu.make_async_copy(t_hbm.at[pl.ds(n * 64, 64)], t_ref.at[n], t_sem.at[n])

    @pl.loop(0, BLOCKS)
    def _(n):
        tensor_load(n).start()

    barrier = pltpu.get_barrier_semaphore()

    def greet(to):
        pl.semaphore_signal(barrier, inc=1, device_id=to, device_id_type=MESH)

    @pl.loop(1, 32)
    def _(n):
        greet(device((z + 2 * (n // 8)) % 8, x, (y + (n // 2) % 4) % 4, (core + n % 2) % 2))

    @pl.loop(0, 8)
    def _(n):
        greet(device((z + 1 + 2 * (n // 2)) % 8, x, y, n % 2))

    @pl.loop(0, 24)
    def _(n):
        greet(device(z, (x + 1 + n // 8) % 4, (n // 2) % 4, n % 2))

    for load in loads:
        load.wait()
    ct = ct_in[...]
    wide_c = ct.astype(f32).T.astype(bf16)
    zero = jnp.zeros((128, 64), bf16)
    weight_c[...] = jnp.concatenate(
        [jnp.concatenate([wide_c, zero], 1), jnp.concatenate([zero, wide_c], 1)], 0
    )
    ct_all[y] = jnp.concatenate([ct, ct], 0)
    b_own = b_in[...].astype(f32)
    b_slots[y, 0:4, :] = jnp.concatenate([b_own, b_own], 1)

    def block_product(n):
        tensor_load(n).wait()
        rows = t_ref[n]
        left = rows[:HALF].reshape(HALF * 16, 128)
        right = rows[HALF:].reshape(HALF * 16, 128)
        prod[n] = jnp.dot(jnp.concatenate([left, right], 1), weight_c[...], preferred_element_type=f32)

    @pl.loop(0, BLOCKS // 2)
    def _(n):
        block_product(n)

    pl.semaphore_wait(barrier, 63)

    def b_copy(n):
        to = (y + n) % 4
        return remote(b_slots.at[y], b_slots.at[y], b_s.at[n], b_r.at[n], device(z, x, to, core))

    def c_copy(n):
        to = (y + n) % 4
        return remote(ct_all.at[y], ct_all.at[y], c_s.at[n], c_r.at[n], device(z, x, to, core))

    for n in (2, 1, 3):
        b_copy(n).start()
    for n in (2, 1, 3):
        c_copy(n).start()

    @pl.loop(BLOCKS // 2, BLOCKS)
    def _(n):
        block_product(n)

    for n in (2, 1, 3):
        b_copy(n).wait()
    for part in range(4):
        b_block[4 * part : 4 * part + 4, :] = b_slots[part, 0:4, :]
    b_all[ja] = b_block[...].astype(bf16)

    row = lax.broadcasted_iota(jnp.int32, (8, 128), 0)

    def target(n):
        return (z_hi + far_first(n // 4)) % 4, (y + far_first(n % 4)) % 4

    def block_sum(n, at_core, out):
        to_z, to_y = target(n)
        block = (to_z * 2 + at_core) * 4 + to_y
        low, high = b_block[0:8, :], b_block[8:16, :]
        for group in range(HALF // 8):
            stack = []
            for pair in range(8):
                start = (group * 8 + pair) * 16
                stack.append(
                    prod[block, start : start + 8, :] * low + prod[block, start + 8 : start + 16, :] * high
                )
            out[n, group * 8 : group * 8 + 8, :] = add_rows(stack, row)

    def core_copy(n):
        return remote(give.at[n], got.at[n], x_s.at[n], x_r.at[n], device(z, x, y, 1 - core))

    @pl.loop(0, 16)
    def _(n):
        block_sum(n, 1 - core, give)
        core_copy(n).start()

    @pl.loop(0, 16)
    def _(n):
        block_sum(n, core, mine)

    def plane_copy(n):
        to_z, to_y = target(n)
        return remote(out_rs.at[n], in_rs.at[n], rs_s.at[n], rs_r.at[n], device(to_z * 2 + z_lo, x, to_y, core))

    @pl.loop(0, 15)
    def _(n):
        core_copy(n).wait()
        out_rs[n] = mine[n] + got[n]
        plane_copy(n).start()

    def ball_copy(n):
        to = (ja + n) % 8
        return remote(
            b_all.at[ja], b_all.at[ja], ball_s.at[n], ball_r.at[n], device((to // 2) * 2 + z_lo, x, y, to % 2)
        )

    for n in range(1, 8):
        ball_copy(n).start()

    for n in (2, 1, 3):
        c_copy(n).wait()
    for n in range(1, 8):
        ball_copy(n).wait()
    b_rows = b_all[...].reshape(128, 128)
    gram_b = lax.dot_general(b_rows, b_rows, (((0,), (0,)), ((), ())), preferred_element_type=f32)
    gram_c = jnp.zeros((128, 128), f32)
    for part in range(4):
        piece = ct_all[part]
        gram_c += lax.dot_general(piece, piece, (((1,), (1,)), ((), ())), preferred_element_type=f32)
    rows2 = lax.broadcasted_iota(jnp.int32, (128, 128), 0)
    cols2 = lax.broadcasted_iota(jnp.int32, (128, 128), 1)
    gram = jnp.where((rows2 < 64) == (cols2 < 64), gram_b * gram_c, 0.0)
    lip = jnp.sqrt(0.5 * jnp.sum(jnp.sum(gram * gram, axis=0, keepdims=True), axis=1, keepdims=True))
    high, low = split(gram / lip)
    both = jnp.concatenate([high, low], 1)
    weight_g[...] = jnp.concatenate([both, both], 0)
    inverse = 1.0 / lip

    tval = jnp.ones((8, 128), f32)
    for step in range(ITERS):
        flag = flags[step].astype(f32)
        tval = flag + (1.0 - flag) * tval
        t_next = (1.0 + jnp.sqrt(1.0 + 4.0 * tval * tval)) / 2.0
        coef[step] = (tval - 1.0) / t_next
        tval = t_next

    start = a_in[...]
    current = jnp.concatenate([start[:HALF], start[HALF:]], 1)

    core_copy(15).wait()
    total = mine[15] + got[15]
    for n in range(15):
        plane_copy(n).wait_recv()
        total = total + in_rs[n]
    target_term = total * inverse

    look = current
    weights = weight_g[...]
    for step in range(ITERS):
        flag = flags[step].astype(f32)
        look = flag * current + (1.0 - flag) * look
        high, low = split(look)
        wide = jnp.dot(jnp.concatenate([high, low], 1), weights, preferred_element_type=f32)
        grad = wide[:, :128] + wide[:, 128:] - target_term
        nxt = jnp.maximum(look - grad, 0.0)
        look = nxt + coef[step, 0:1, :] * (nxt - current)
        current = nxt

    turned = pltpu.roll(current, 64, 1)
    high, low = split(jnp.concatenate([current, turned], 0))
    gram_a = lax.dot_general(
        jnp.concatenate([high, low, high], 0),
        jnp.concatenate([high, high, low], 0),
        (((0,), (0,)), ((), ())),
        preferred_element_type=f32,
    )
    lane = lax.broadcasted_iota(jnp.int32, (HALF, 128), 1)
    packed = jnp.where(lane < 64, gram_a[0:32], gram_a[96:128])
    gram_out[0] = packed[:16]
    gram_out[1] = packed[16:]

    def z_peer(n):
        return (z + 4 + n // 2) % 8, (core + n % 2) % 2

    def z_copy(n):
        to_z, to_core = z_peer(n)
        return remote(gram_out.at[to_core], gram_z.at[core, z], z_s.at[n], z_r.at[n], device(to_z, x, y, to_core))

    for n in range(16):
        if n != 8:
            z_copy(n).start()
    gram_z[core, z] = gram_out[core]
    up_ref[0:HALF, :] = current[:, :64]
    up_ref[HALF:, :] = current[:, 64:]
    for n in range(16):
        if n != 8:
            z_copy(n).wait_recv()
    half = gram_z[0, 0]
    for n in range(1, 16):
        half = half + gram_z[n // 8, n % 8]
    gram_half[...] = half

    def xy_copy(n):
        to_x, to_y = (x + far_first(n // 8)) % 4, (y + far_first((n // 2) % 4)) % 4
        to_core = (core + n % 2) % 2
        return remote(
            gram_half, gram_xy.at[core, x * 4 + y], xy_s.at[n], xy_r.at[n], device(z, to_x, to_y, to_core)
        )

    for n in range(32):
        if n != 30:
            xy_copy(n).start()
    gram_xy[core, x * 4 + y] = half
    for n in range(32):
        if n != 30:
            xy_copy(n).wait_recv()
    for part in range(2):
        whole = gram_xy[part, 0]
        for n in range(1, 16):
            whole = whole + gram_xy[part, n]
        gram_ref[16 * part : 16 * part + 16, :] = whole[:, :64]
        gram_ref[HALF + 16 * part : HALF + 16 * part + 16, :] = whole[:, 64:]

    @pl.loop(0, 15)
    def _(n):
        plane_copy(n).wait_send()

    for n in range(16):
        if n != 8:
            z_copy(n).wait_send()
    for n in range(32):
        if n != 30:
            xy_copy(n).wait_send()


def shards(tensor, factor_b, factor_c, factor_a, restart):
    f32, bf16 = jnp.float32, jnp.bfloat16
    dma = pltpu.SemaphoreType.DMA
    return pl.pallas_call(
        kernel,
        out_shape=(
            jax.ShapeDtypeStruct((64, 64), f32),
            jax.ShapeDtypeStruct((64, 64), f32),
        ),
        in_specs=[pl.BlockSpec(memory_space=pl.ANY)] * 5,
        out_specs=[pl.BlockSpec(memory_space=pltpu.VMEM)] * 2,
        scratch_shapes=[
            pltpu.VMEM((BLOCKS, 64, 16, 128), bf16),
            pltpu.VMEM((BLOCKS, 512, 128), f32),
            pltpu.VMEM((4, 64), bf16),
            pltpu.VMEM((64, 128), bf16),
            pltpu.VMEM((64, 64), f32),
            pltpu.SMEM((ITERS,), jnp.int32),
            pltpu.VMEM((4, 8, 128), f32),
            pltpu.VMEM((16, 128), f32),
            pltpu.VMEM((8, 16, 128), bf16),
            pltpu.VMEM((4, 128, 128), bf16),
            pltpu.VMEM((256, 128), bf16),
            pltpu.VMEM((16, HALF, 128), f32),
            pltpu.VMEM((16, HALF, 128), f32),
            pltpu.VMEM((16, HALF, 128), f32),
            pltpu.VMEM((16, HALF, 128), f32),
            pltpu.VMEM((16, HALF, 128), f32),
            pltpu.VMEM((256, 256), bf16),
            pltpu.VMEM((ITERS, 8, 128), f32),
            pltpu.VMEM((2, 16, 128), f32),
            pltpu.VMEM((2, 8, 16, 128), f32),
            pltpu.VMEM((16, 128), f32),
            pltpu.VMEM((2, 16, 16, 128), f32),
            dma((BLOCKS,)), dma((4,)), dma((4,)), dma((4,)), dma((4,)), dma((4,)), dma((8,)), dma((8,)),
            dma((16,)), dma((16,)), dma((16,)), dma((16,)), dma((16,)), dma((16,)), dma((32,)), dma((32,)),
        ],
        compiler_params=pltpu.CompilerParams(
            collective_id=0, has_side_effects=True, vmem_limit_bytes=56 * 2**20
        ),
        name="cp_update",
    )(tensor, factor_b, factor_c.T, factor_a, restart)


def solution(mesh):
    return jax.shard_map(
        shards,
        mesh=mesh,
        in_specs=(
            P("ia", "ja", "ka"),
            P(("ja", "ka"), None),
            P("ka", None),
            P(("ia", "ja", "ka"), None),
            P(),
        ),
        out_specs=(P(("ia", "ja", "ka"), None), P()),
        check_vma=False,
    )
```

time: 422 us -> 49.3 us (0.12)
  blocking collectives: 239 us -> 0 us
  waiting for transfers between devices: 135 us -> 0 us
  Pallas kernels: 0 us -> 45.7 us
  between operations: 14.8 us -> 0.64 us
  matrix products: 12.3 us -> 0 us
  loops' own time: 9.95 us -> 0 us
  local copies, waits for them, and re-layouts: 9.79 us -> 2.75 us
    psum x3 -> x0, blocking collectives: 230 us -> none  [the longest x1 137 us: shards(): gram_b = lax.psum(local_b, ('ja', 'ka'))]
    psum x1 -> x0, waiting for transfers between devices: 135 us -> none  [shards(): lax.psum(jnp.sum(partial_value * b_wide[None, :, :], axis=1), ('ja', 'ka'))]
    pallas_call x0 -> x1, Pallas kernels: none -> 45.7 us  [shards(): pl.pallas_call(kernel, out_shape=(jax.ShapeDtypeStruct((64, 64), f32), ja...]
    dot_general x16 -> x0, matrix products: 12.3 us -> none  [the longest x1 9.65 us: shards(): jnp.dot(tensor.reshape(rows * cols, depth), factor_c, preferred_element_t...]
    another operation x1 -> x0, loops' own time: 9.95 us -> none  [shards(): lax.fori_loop(0, ITERS, one_step, (factor_a, factor_a, jnp.float32(1.0)))]
    all_gather x1 -> x0, blocking collectives: 9.02 us -> none  [shards(): b_block = lax.all_gather(factor_b, 'ka', axis=0, tiled=True)]
    dynamic_slice x13 -> x0, local copies, waits for them, and re-layouts: 8.83 us -> none  [the longest x12 8 us: one_step(): flag = restart[step].astype(jnp.float32)]
  transfers between devices with their start and end apart: 1 -> 0, of which waited for: 1 -> 0; matrix products, arithmetic and copies ran while one was open for 0% -> 0% of each run, Pallas kernels for 0% -> 0%
where the time goes in v1:
time: 49.3 us; the launch traced here: 49.1 us
  Pallas kernels  45.7 us (93%)
  local copies, waits for them, and re-layouts  2.75 us (6%)
  between operations  0.64 us (1%)
    pallas_call x1, Pallas kernels, shards(): pl.pallas_call(kernel, out_shape=(jax.ShapeDtypeStruct((64, 64), f32), ja...  45.7 us
    unnamed x2, local copies, waits for them, and re-layouts  2.75 us

profile of v1, /device:TPU:1, one launch (start us, length us, event | category | flops | bytes accessed | tf_op | source)
XLA Modules:
  0.0 49.1 jit_solution(11097801299650021216)
XLA Ops:
  0.6 45.7 %cp_update.1 = (f32[64,64]{1,0:T(8,128)}, f32[64,64]{1,0:T(8,128)}) custom-call(bf16[2048,16,128]{2,1,0:T(8,128)(2,1)} %t_hbm.1, bf16[4,64]{1,0:T(4,128)(2,1)} %b_hbm.1, bf16[64,128]{1,0:T(8,128)(2,1)} %bitcast.1, f32[64,64]{1,0:T(8,128)} %a_hbm.1, s32[12]{0:T(128)} %restart_hbm.1), custom_call_target="tpu_custom_call" | custom-call | tf_op jit(solution)/shard_map/cp_update/pallas_call | solution.py:306
  46.3 1.4 %copy.9 = f32[64,64]{1,0:T(8,128)} copy(f32[64,64]{1,0:T(8,128)} %get-tuple-element.4) | data formatting | bytes 32768
  47.7 1.4 %copy.10 = f32[64,64]{1,0:T(8,128)} copy(f32[64,64]{1,0:T(8,128)} %get-tuple-element.5) | data formatting | bytes 32768

commit v2 on v1

--- a/solution.py
+++ b/solution.py
@@ -10,7 +10,10 @@
 ITERS = 12
 MESH = pl.DeviceIdType.MESH
 BLOCKS = 32
+GROUP = 8
 HALF = 32
+
+B, C, B_ALL, CORE, PLANE, Z, XY, KINDS = range(8)
 
 
 def far_first(n):
@@ -38,8 +41,7 @@
     b_slots, b_block, b_all, ct_all, weight_c,
     give, got, mine, out_rs, in_rs, weight_g, coef,
     gram_out, gram_z, gram_half, gram_xy,
-    t_sem, in_sem, b_s, b_r, c_s, c_r, ball_s, ball_r,
-    x_s, x_r, rs_s, rs_r, z_s, z_r, xy_s, xy_r,
+    t_sem, in_sem, core_r, sent, got_all,
 ):
     f32, bf16 = jnp.float32, jnp.bfloat16
     ia, ja, y = lax.axis_index("ia"), lax.axis_index("ja"), lax.axis_index("ka")
@@ -53,6 +55,9 @@
         return pltpu.make_async_remote_copy(
             src_ref=src, dst_ref=dst, send_sem=send, recv_sem=recv, device_id=to, device_id_type=MESH
         )
+
+    def exchange(ref, kind):
+        return remote(ref, ref, sent.at[kind], got_all.at[kind], device(z, x, y, 1 - core))
 
     loads = [
         pltpu.make_async_copy(b_hbm, b_in, in_sem.at[0]),
@@ -64,11 +69,11 @@
         load.start()
 
     def tensor_load(n):
-        return pltpu.make_async_copy(t_hbm.at[pl.ds(n * 64, 64)], t_ref.at[n], t_sem.at[n])
-
-    @pl.loop(0, BLOCKS)
-    def _(n):
-        tensor_load(n).start()
+        rows = pl.ds(n * GROUP * 64, GROUP * 64)
+        return pltpu.make_async_copy(t_hbm.at[rows], t_ref.at[rows], t_sem.at[n])
+
+    for n in range(BLOCKS // GROUP):
+        tensor_load(n).start(priority=n % 2)
 
     barrier = pltpu.get_barrier_semaphore()
 
@@ -99,38 +104,36 @@
     b_own = b_in[...].astype(f32)
     b_slots[y, 0:4, :] = jnp.concatenate([b_own, b_own], 1)
 
-    def block_product(n):
+    def product(n):
         tensor_load(n).wait()
-        rows = t_ref[n]
-        left = rows[:HALF].reshape(HALF * 16, 128)
-        right = rows[HALF:].reshape(HALF * 16, 128)
-        prod[n] = jnp.dot(jnp.concatenate([left, right], 1), weight_c[...], preferred_element_type=f32)
-
-    @pl.loop(0, BLOCKS // 2)
-    def _(n):
-        block_product(n)
+        rows = t_ref[pl.ds(n * GROUP * 64, GROUP * 64)].reshape(GROUP, 64, 16, 128)
+        left = rows[:, :HALF].reshape(GROUP * HALF * 16, 128)
+        right = rows[:, HALF:].reshape(GROUP * HALF * 16, 128)
+        out = jnp.dot(jnp.concatenate([left, right], 1), weight_c[...], preferred_element_type=f32)
+        prod[pl.ds(n * GROUP, GROUP)] = out.reshape(GROUP, HALF * 16, 128)
+
+    @pl.loop(0, BLOCKS // GROUP - 1)
+    def _(n):
+        product(n)
 
     pl.semaphore_wait(barrier, 63)
 
     def b_copy(n):
         to = (y + n) % 4
-        return remote(b_slots.at[y], b_slots.at[y], b_s.at[n], b_r.at[n], device(z, x, to, core))
+        return remote(b_slots.at[y], b_slots.at[y], sent.at[B], got_all.at[B], device(z, x, to, core))
 
     def c_copy(n):
         to = (y + n) % 4
-        return remote(ct_all.at[y], ct_all.at[y], c_s.at[n], c_r.at[n], device(z, x, to, core))
+        return remote(ct_all.at[y], ct_all.at[y], sent.at[C], got_all.at[C], device(z, x, to, core))
 
     for n in (2, 1, 3):
         b_copy(n).start()
     for n in (2, 1, 3):
         c_copy(n).start()
 
-    @pl.loop(BLOCKS // 2, BLOCKS)
-    def _(n):
-        block_product(n)
-
-    for n in (2, 1, 3):
-        b_copy(n).wait()
+    product(BLOCKS // GROUP - 1)
+
+    exchange(b_slots.at[0:3], B).wait()
     for part in range(4):
         b_block[4 * part : 4 * part + 4, :] = b_slots[part, 0:4, :]
     b_all[ja] = b_block[...].astype(bf16)
@@ -154,7 +157,7 @@
             out[n, group * 8 : group * 8 + 8, :] = add_rows(stack, row)
 
     def core_copy(n):
-        return remote(give.at[n], got.at[n], x_s.at[n], x_r.at[n], device(z, x, y, 1 - core))
+        return remote(give.at[n], got.at[n], sent.at[CORE], core_r.at[n // 4], device(z, x, y, 1 - core))
 
     @pl.loop(0, 16)
     def _(n):
@@ -167,27 +170,30 @@
 
     def plane_copy(n):
         to_z, to_y = target(n)
-        return remote(out_rs.at[n], in_rs.at[n], rs_s.at[n], rs_r.at[n], device(to_z * 2 + z_lo, x, to_y, core))
-
-    @pl.loop(0, 15)
-    def _(n):
-        core_copy(n).wait()
-        out_rs[n] = mine[n] + got[n]
-        plane_copy(n).start()
+        return remote(
+            out_rs.at[n], in_rs.at[n], sent.at[PLANE], got_all.at[PLANE], device(to_z * 2 + z_lo, x, to_y, core)
+        )
+
+    for part in range(4):
+        blocks = got.at[4 * part : 4 * part + 4]
+        remote(blocks, blocks, sent.at[CORE], core_r.at[part], device(z, x, y, 1 - core)).wait_recv()
+
+        @pl.loop(4 * part, min(4 * part + 4, 15))
+        def _(n):
+            out_rs[n] = mine[n] + got[n]
+            plane_copy(n).start()
 
     def ball_copy(n):
         to = (ja + n) % 8
         return remote(
-            b_all.at[ja], b_all.at[ja], ball_s.at[n], ball_r.at[n], device((to // 2) * 2 + z_lo, x, y, to % 2)
+            b_all.at[ja], b_all.at[ja], sent.at[B_ALL], got_all.at[B_ALL], device((to // 2) * 2 + z_lo, x, y, to % 2)
         )
 
     for n in range(1, 8):
         ball_copy(n).start()
 
-    for n in (2, 1, 3):
-        c_copy(n).wait()
-    for n in range(1, 8):
-        ball_copy(n).wait()
+    exchange(ct_all.at[0:3], C).wait()
+    exchange(b_all.at[0:7], B_ALL).wait()
     b_rows = b_all[...].reshape(128, 128)
     gram_b = lax.dot_general(b_rows, b_rows, (((0,), (0,)), ((), ())), preferred_element_type=f32)
     gram_c = jnp.zeros((128, 128), f32)
@@ -214,10 +220,9 @@
     start = a_in[...]
     current = jnp.concatenate([start[:HALF], start[HALF:]], 1)
 
-    core_copy(15).wait()
     total = mine[15] + got[15]
+    exchange(in_rs.at[0:15], PLANE).wait_recv()
     for n in range(15):
-        plane_copy(n).wait_recv()
         total = total + in_rs[n]
     target_term = total * inverse
 
@@ -247,72 +252,79 @@
     gram_out[1] = packed[16:]
 
     def z_peer(n):
-        return (z + 4 + n // 2) % 8, (core + n % 2) % 2
+        step = (4, 3, 5, 2, 6, 1, 7, 0)[n // 2]
+        return (z + step) % 8, (core + n % 2) % 2
 
     def z_copy(n):
         to_z, to_core = z_peer(n)
-        return remote(gram_out.at[to_core], gram_z.at[core, z], z_s.at[n], z_r.at[n], device(to_z, x, y, to_core))
+        return remote(
+            gram_out.at[to_core], gram_z.at[core * 8 + z], sent.at[Z], got_all.at[Z], device(to_z, x, y, to_core)
+        )
 
     for n in range(16):
-        if n != 8:
+        if n != 14:
             z_copy(n).start()
-    gram_z[core, z] = gram_out[core]
+    gram_z[core * 8 + z] = gram_out[core]
     up_ref[0:HALF, :] = current[:, :64]
     up_ref[HALF:, :] = current[:, 64:]
-    for n in range(16):
-        if n != 8:
-            z_copy(n).wait_recv()
-    half = gram_z[0, 0]
+    exchange(gram_z.at[0:15], Z).wait_recv()
+    half = gram_z[0]
     for n in range(1, 16):
-        half = half + gram_z[n // 8, n % 8]
+        half = half + gram_z[n]
     gram_half[...] = half
 
     def xy_copy(n):
-        to_x, to_y = (x + far_first(n // 8)) % 4, (y + far_first((n // 2) % 4)) % 4
+        step = (10, 11, 9, 14, 6, 8, 2, 15, 13, 7, 5, 12, 4, 3, 1, 0)[n // 2]
+        to_x, to_y = (x + step // 4) % 4, (y + step % 4) % 4
         to_core = (core + n % 2) % 2
         return remote(
-            gram_half, gram_xy.at[core, x * 4 + y], xy_s.at[n], xy_r.at[n], device(z, to_x, to_y, to_core)
+            gram_half, gram_xy.at[core * 16 + x * 4 + y], sent.at[XY], got_all.at[XY], device(z, to_x, to_y, to_core)
         )
 
     for n in range(32):
         if n != 30:
             xy_copy(n).start()
-    gram_xy[core, x * 4 + y] = half
-    for n in range(32):
-        if n != 30:
-            xy_copy(n).wait_recv()
+    gram_xy[core * 16 + x * 4 + y] = half
+    exchange(gram_xy.at[0:31], XY).wait_recv()
     for part in range(2):
-        whole = gram_xy[part, 0]
+        whole = gram_xy[16 * part]
         for n in range(1, 16):
-            whole = whole + gram_xy[part, n]
+            whole = whole + gram_xy[16 * part + n]
         gram_ref[16 * part : 16 * part + 16, :] = whole[:, :64]
         gram_ref[HALF + 16 * part : HALF + 16 * part + 16, :] = whole[:, 64:]
 
-    @pl.loop(0, 15)
-    def _(n):
-        plane_copy(n).wait_send()
-
-    for n in range(16):
-        if n != 8:
-            z_copy(n).wait_send()
-    for n in range(32):
-        if n != 30:
-            xy_copy(n).wait_send()
+    exchange(give, CORE).wait_send()
+    exchange(out_rs.at[0:15], PLANE).wait_send()
+    exchange(gram_z.at[0:15], Z).wait_send()
+    exchange(gram_xy.at[0:31], XY).wait_send()
+
+
+def write_out(up_ref, gram_ref, up_hbm, gram_hbm, sem):
+    copies = [
+        pltpu.make_async_copy(up_ref, up_hbm, sem.at[0]),
+        pltpu.make_async_copy(gram_ref, gram_hbm, sem.at[1]),
+    ]
+    for copy in copies:
+        copy.start()
+    for copy in copies:
+        copy.wait()
 
 
 def shards(tensor, factor_b, factor_c, factor_a, restart):
     f32, bf16 = jnp.float32, jnp.bfloat16
     dma = pltpu.SemaphoreType.DMA
-    return pl.pallas_call(
+    result = jax.ShapeDtypeStruct((64, 64), f32)
+    operands = [
+        pltpu.with_memory_space_constraint(array, pltpu.HBM)
+        for array in (tensor, factor_b, factor_c.T, factor_a, restart)
+    ]
+    updated, gram_a = pl.pallas_call(
         kernel,
-        out_shape=(
-            jax.ShapeDtypeStruct((64, 64), f32),
-            jax.ShapeDtypeStruct((64, 64), f32),
-        ),
-        in_specs=[pl.BlockSpec(memory_space=pl.ANY)] * 5,
+        out_shape=(pltpu.VMEM((64, 64), f32), pltpu.VMEM((64, 64), f32)),
+        in_specs=[pl.BlockSpec(memory_space=pltpu.HBM)] * 5,
         out_specs=[pl.BlockSpec(memory_space=pltpu.VMEM)] * 2,
         scratch_shapes=[
-            pltpu.VMEM((BLOCKS, 64, 16, 128), bf16),
+            pltpu.VMEM((BLOCKS * 64, 16, 128), bf16),
             pltpu.VMEM((BLOCKS, 512, 128), f32),
             pltpu.VMEM((4, 64), bf16),
             pltpu.VMEM((64, 128), bf16),
@@ -331,17 +343,24 @@
             pltpu.VMEM((256, 256), bf16),
             pltpu.VMEM((ITERS, 8, 128), f32),
             pltpu.VMEM((2, 16, 128), f32),
-            pltpu.VMEM((2, 8, 16, 128), f32),
+            pltpu.VMEM((16, 16, 128), f32),
             pltpu.VMEM((16, 128), f32),
-            pltpu.VMEM((2, 16, 16, 128), f32),
-            dma((BLOCKS,)), dma((4,)), dma((4,)), dma((4,)), dma((4,)), dma((4,)), dma((8,)), dma((8,)),
-            dma((16,)), dma((16,)), dma((16,)), dma((16,)), dma((16,)), dma((16,)), dma((32,)), dma((32,)),
+            pltpu.VMEM((32, 16, 128), f32),
+            dma((BLOCKS // GROUP,)), dma((4,)), dma((4,)), dma((KINDS,)), dma((KINDS,)),
         ],
         compiler_params=pltpu.CompilerParams(
-            collective_id=0, has_side_effects=True, vmem_limit_bytes=56 * 2**20
+            collective_id=0, has_side_effects=True, vmem_limit_bytes=32 * 2**20
         ),
         name="cp_update",
-    )(tensor, factor_b, factor_c.T, factor_a, restart)
+    )(*operands)
+    return pl.pallas_call(
+        write_out,
+        out_shape=(result, result),
+        in_specs=[pl.BlockSpec(memory_space=pltpu.VMEM)] * 2,
+        out_specs=[pl.BlockSpec(memory_space=pltpu.HBM)] * 2,
+        scratch_shapes=[dma((2,))],
+        name="write_out",
+    )(*(pltpu.with_memory_space_constraint(array, pltpu.VMEM) for array in (updated, gram_a)))
 
 
 def solution(mesh):

time: 49.3 us -> 42.8 us (0.87)
  Pallas kernels: 45.7 us -> 42 us
  local copies, waits for them, and re-layouts: 2.75 us -> 0 us
    pallas_call x1 -> x2, Pallas kernels: 45.7 us -> 42 us  [the longest x1 41.4 us: shards(): pl.pallas_call(kernel, out_shape=(pltpu.VMEM((64, 64), f32), pltpu.VMEM((...]
    unnamed x2 -> x0, local copies, waits for them, and re-layouts: 2.75 us -> none
where the time goes in v2:
time: 42.8 us; the launch traced here: 42.7 us
  Pallas kernels  42 us (98%)
  between operations  0.64 us (1%)
    pallas_call x1, Pallas kernels, shards(): pl.pallas_call(kernel, out_shape=(pltpu.VMEM((64, 64), f32), pltpu.VMEM((...  41.4 us

profile of v2, /device:TPU:1, one launch (start us, length us, event | category | flops | bytes accessed | tf_op | source)
XLA Modules:
  0.0 42.7 jit_solution(7297941049831733129)
XLA Ops:
  0.6 41.4 %cp_update.1 = (f32[64,64]{1,0:T(8,128)S(1)}, f32[64,64]{1,0:T(8,128)S(1)}) custom-call(bf16[2048,16,128]{2,1,0:T(8,128)(2,1)} %t_hbm.1, bf16[4,64]{1,0:T(4,128)(2,1)} %b_hbm.1, bf16[64,128]{1,0:T(8,128)(2,1)} %bitcast.1, f32[64,64]{1,0:T(8,128)} %a_hbm.1, s32[12]{0:T(128)} %restart_hbm.1), custom_call_target="tpu_custom_call" | custom-call | tf_op jit(solution)/shard_map/cp_update/pallas_call | solution.py:321
  42.0 0.6 %write_out.1 = (f32[64,64]{1,0:T(8,128)}, f32[64,64]{1,0:T(8,128)}) custom-call(f32[64,64]{1,0:T(8,128)S(1)} %get-tuple-element.4.up_ref, f32[64,64]{1,0:T(8,128)S(1)} %get-tuple-element.5.gram_ref), custom_call_target="tpu_custom_call" | custom-call | tf_op jit(solution)/shard_map/write_out/pallas_call | solution.py:356

commit v3 on v2

--- a/solution.py
+++ b/solution.py
@@ -12,8 +12,9 @@
 BLOCKS = 32
 GROUP = 8
 HALF = 32
-
-B, C, B_ALL, CORE, PLANE, Z, XY, KINDS = range(8)
+OFFSET = 32767
+STEPS = 2.0 * OFFSET
+B, C, B_ALL, CORE, PLANE, PLANE_STEP, Z, XY, KINDS = range(9)
 
 
 def far_first(n):
@@ -30,6 +31,16 @@
     return stack[0]
 
 
+def encode(value):
+    top = jnp.maximum(jnp.max(value, axis=0, keepdims=True), 2e-34)
+    codes = (value * (STEPS / top) + 0.5).astype(jnp.int32) - OFFSET
+    return codes.astype(jnp.int16), top * (1.0 / STEPS)
+
+
+def decode(codes, step):
+    return (codes.astype(jnp.int32).astype(jnp.float32) + OFFSET) * step
+
+
 def split(value):
     high = value.astype(jnp.bfloat16)
     return high, (value - high.astype(jnp.float32)).astype(jnp.bfloat16)
@@ -39,7 +50,7 @@
     t_hbm, b_hbm, ct_hbm, a_hbm, restart_hbm, up_ref, gram_ref,
     t_ref, prod, b_in, ct_in, a_in, flags,
     b_slots, b_block, b_all, ct_all, weight_c,
-    give, got, mine, out_rs, in_rs, weight_g, coef,
+    give, got, mine, out_rs, in_rs, out_step, in_step, weight_g, coef,
     gram_out, gram_z, gram_half, gram_xy,
     t_sem, in_sem, core_r, sent, got_all,
 ):
@@ -112,9 +123,6 @@
         out = jnp.dot(jnp.concatenate([left, right], 1), weight_c[...], preferred_element_type=f32)
         prod[pl.ds(n * GROUP, GROUP)] = out.reshape(GROUP, HALF * 16, 128)
 
-    @pl.loop(0, BLOCKS // GROUP - 1)
-    def _(n):
-        product(n)
 
     pl.semaphore_wait(barrier, 63)
 
@@ -131,7 +139,9 @@
     for n in (2, 1, 3):
         c_copy(n).start()
 
-    product(BLOCKS // GROUP - 1)
+    @pl.loop(0, BLOCKS // GROUP)
+    def _(n):
+        product(n)
 
     exchange(b_slots.at[0:3], B).wait()
     for part in range(4):
@@ -168,11 +178,9 @@
     def _(n):
         block_sum(n, core, mine)
 
-    def plane_copy(n):
+    def plane_copy(n, src, dst, kind):
         to_z, to_y = target(n)
-        return remote(
-            out_rs.at[n], in_rs.at[n], sent.at[PLANE], got_all.at[PLANE], device(to_z * 2 + z_lo, x, to_y, core)
-        )
+        return remote(src.at[n], dst.at[n], sent.at[kind], got_all.at[kind], device(to_z * 2 + z_lo, x, to_y, core))
 
     for part in range(4):
         blocks = got.at[4 * part : 4 * part + 4]
@@ -180,8 +188,9 @@
 
         @pl.loop(4 * part, min(4 * part + 4, 15))
         def _(n):
-            out_rs[n] = mine[n] + got[n]
-            plane_copy(n).start()
+            out_rs[n], out_step[n] = encode(mine[n] + got[n])
+            plane_copy(n, out_rs, in_rs, PLANE).start()
+            plane_copy(n, out_step, in_step, PLANE_STEP).start()
 
     def ball_copy(n):
         to = (ja + n) % 8
@@ -221,9 +230,10 @@
     current = jnp.concatenate([start[:HALF], start[HALF:]], 1)
 
     total = mine[15] + got[15]
+    exchange(in_step.at[0:15], PLANE_STEP).wait_recv()
     exchange(in_rs.at[0:15], PLANE).wait_recv()
     for n in range(15):
-        total = total + in_rs[n]
+        total = total + decode(in_rs[n], in_step[n])
     target_term = total * inverse
 
     look = current
@@ -295,6 +305,7 @@
 
     exchange(give, CORE).wait_send()
     exchange(out_rs.at[0:15], PLANE).wait_send()
+    exchange(out_step.at[0:15], PLANE_STEP).wait_send()
     exchange(gram_z.at[0:15], Z).wait_send()
     exchange(gram_xy.at[0:31], XY).wait_send()
 
@@ -338,8 +349,10 @@
             pltpu.VMEM((16, HALF, 128), f32),
             pltpu.VMEM((16, HALF, 128), f32),
             pltpu.VMEM((16, HALF, 128), f32),
-            pltpu.VMEM((16, HALF, 128), f32),
-            pltpu.VMEM((16, HALF, 128), f32),
+            pltpu.VMEM((16, HALF, 128), jnp.int16),
+            pltpu.VMEM((16, HALF, 128), jnp.int16),
+            pltpu.VMEM((16, 1, 128), f32),
+            pltpu.VMEM((16, 1, 128), f32),
             pltpu.VMEM((256, 256), bf16),
             pltpu.VMEM((ITERS, 8, 128), f32),
             pltpu.VMEM((2, 16, 128), f32),

time: 42.8 us -> 40.3 us (0.942)
  Pallas kernels: 42 us -> 39.6 us
    pallas_call x1, Pallas kernels: 41.4 us -> 38.9 us  [shards(): pl.pallas_call(kernel, out_shape=(pltpu.VMEM((64, 64), f32), pltpu.VMEM((...]
where the time goes in v3:
time: 40.3 us; the launch traced here: 40.2 us
  Pallas kernels  39.6 us (98%)
  between operations  0.64 us (2%)
    pallas_call x1, Pallas kernels, shards(): pl.pallas_call(kernel, out_shape=(pltpu.VMEM((64, 64), f32), pltpu.VMEM((...  38.9 us

profile of v3, /device:TPU:1, one launch (start us, length us, event | category | flops | bytes accessed | tf_op | source)
XLA Modules:
  0.0 40.2 jit_solution(4148718741630991248)
XLA Ops:
  0.6 38.9 %cp_update.1 = (f32[64,64]{1,0:T(8,128)S(1)}, f32[64,64]{1,0:T(8,128)S(1)}) custom-call(bf16[2048,16,128]{2,1,0:T(8,128)(2,1)} %t_hbm.1, bf16[4,64]{1,0:T(4,128)(2,1)} %b_hbm.1, bf16[64,128]{1,0:T(8,128)(2,1)} %bitcast.1, f32[64,64]{1,0:T(8,128)} %a_hbm.1, s32[12]{0:T(128)} %restart_hbm.1), custom_call_target="tpu_custom_call" | custom-call | tf_op jit(solution)/shard_map/cp_update/pallas_call | solution.py:332
  39.6 0.6 %write_out.1 = (f32[64,64]{1,0:T(8,128)}, f32[64,64]{1,0:T(8,128)}) custom-call(f32[64,64]{1,0:T(8,128)S(1)} %get-tuple-element.4.up_ref, f32[64,64]{1,0:T(8,128)S(1)} %get-tuple-element.5.gram_ref), custom_call_target="tpu_custom_call" | custom-call | tf_op jit(solution)/shard_map/write_out/pallas_call | solution.py:369

commit v4 on v3

--- a/solution.py
+++ b/solution.py
@@ -14,7 +14,7 @@
 HALF = 32
 OFFSET = 32767
 STEPS = 2.0 * OFFSET
-B, C, B_ALL, CORE, PLANE, PLANE_STEP, Z, XY, KINDS = range(9)
+B, C, B_ALL, CORE, PLANE, PLANE_STEP, Z, Z_STEP, XY, XY_STEP, KINDS = range(11)
 
 
 def far_first(n):
@@ -52,6 +52,7 @@
     b_slots, b_block, b_all, ct_all, weight_c,
     give, got, mine, out_rs, in_rs, out_step, in_step, weight_g, coef,
     gram_out, gram_z, gram_half, gram_xy,
+    gram_step, gram_z_step, half_step, gram_xy_step,
     t_sem, in_sem, core_r, sent, got_all,
 ):
     f32, bf16 = jnp.float32, jnp.bfloat16
@@ -258,48 +259,54 @@
     )
     lane = lax.broadcasted_iota(jnp.int32, (HALF, 128), 1)
     packed = jnp.where(lane < 64, gram_a[0:32], gram_a[96:128])
-    gram_out[0] = packed[:16]
-    gram_out[1] = packed[16:]
+    gram_out[0], gram_step[0] = encode(packed[:16])
+    gram_out[1], gram_step[1] = encode(packed[16:])
 
     def z_peer(n):
         step = (4, 3, 5, 2, 6, 1, 7, 0)[n // 2]
         return (z + step) % 8, (core + n % 2) % 2
 
-    def z_copy(n):
+    def z_copy(n, src, dst, kind):
         to_z, to_core = z_peer(n)
         return remote(
-            gram_out.at[to_core], gram_z.at[core * 8 + z], sent.at[Z], got_all.at[Z], device(to_z, x, y, to_core)
+            src.at[to_core], dst.at[core * 8 + z], sent.at[kind], got_all.at[kind], device(to_z, x, y, to_core)
         )
 
     for n in range(16):
         if n != 14:
-            z_copy(n).start()
+            z_copy(n, gram_out, gram_z, Z).start()
+            z_copy(n, gram_step, gram_z_step, Z_STEP).start()
     gram_z[core * 8 + z] = gram_out[core]
+    gram_z_step[core * 8 + z] = gram_step[core]
     up_ref[0:HALF, :] = current[:, :64]
     up_ref[HALF:, :] = current[:, 64:]
     exchange(gram_z.at[0:15], Z).wait_recv()
-    half = gram_z[0]
+    exchange(gram_z_step.at[0:15], Z_STEP).wait_recv()
+    half = decode(gram_z[0], gram_z_step[0])
     for n in range(1, 16):
-        half = half + gram_z[n]
-    gram_half[...] = half
-
-    def xy_copy(n):
+        half = half + decode(gram_z[n], gram_z_step[n])
+    gram_half[...], half_step[...] = encode(half)
+
+    def xy_copy(n, src, dst, kind):
         step = (10, 11, 9, 14, 6, 8, 2, 15, 13, 7, 5, 12, 4, 3, 1, 0)[n // 2]
         to_x, to_y = (x + step // 4) % 4, (y + step % 4) % 4
         to_core = (core + n % 2) % 2
         return remote(
-            gram_half, gram_xy.at[core * 16 + x * 4 + y], sent.at[XY], got_all.at[XY], device(z, to_x, to_y, to_core)
+            src, dst.at[core * 16 + x * 4 + y], sent.at[kind], got_all.at[kind], device(z, to_x, to_y, to_core)
         )
 
     for n in range(32):
         if n != 30:
-            xy_copy(n).start()
-    gram_xy[core * 16 + x * 4 + y] = half
+            xy_copy(n, gram_half, gram_xy, XY).start()
+            xy_copy(n, half_step, gram_xy_step, XY_STEP).start()
+    gram_xy[core * 16 + x * 4 + y] = gram_half[...]
+    gram_xy_step[core * 16 + x * 4 + y] = half_step[...]
     exchange(gram_xy.at[0:31], XY).wait_recv()
+    exchange(gram_xy_step.at[0:31], XY_STEP).wait_recv()
     for part in range(2):
-        whole = gram_xy[16 * part]
+        whole = decode(gram_xy[16 * part], gram_xy_step[16 * part])
         for n in range(1, 16):
-            whole = whole + gram_xy[16 * part + n]
+            whole = whole + decode(gram_xy[16 * part + n], gram_xy_step[16 * part + n])
         gram_ref[16 * part : 16 * part + 16, :] = whole[:, :64]
         gram_ref[HALF + 16 * part : HALF + 16 * part + 16, :] = whole[:, 64:]
 
@@ -307,7 +314,9 @@
     exchange(out_rs.at[0:15], PLANE).wait_send()
     exchange(out_step.at[0:15], PLANE_STEP).wait_send()
     exchange(gram_z.at[0:15], Z).wait_send()
+    exchange(gram_z_step.at[0:15], Z_STEP).wait_send()
     exchange(gram_xy.at[0:31], XY).wait_send()
+    exchange(gram_xy_step.at[0:31], XY_STEP).wait_send()
 
 
 def write_out(up_ref, gram_ref, up_hbm, gram_hbm, sem):
@@ -355,10 +364,14 @@
             pltpu.VMEM((16, 1, 128), f32),
             pltpu.VMEM((256, 256), bf16),
             pltpu.VMEM((ITERS, 8, 128), f32),
-            pltpu.VMEM((2, 16, 128), f32),
-            pltpu.VMEM((16, 16, 128), f32),
-            pltpu.VMEM((16, 128), f32),
-            pltpu.VMEM((32, 16, 128), f32),
+            pltpu.VMEM((2, 16, 128), jnp.int16),
+            pltpu.VMEM((16, 16, 128), jnp.int16),
+            pltpu.VMEM((16, 128), jnp.int16),
+            pltpu.VMEM((32, 16, 128), jnp.int16),
+            pltpu.VMEM((2, 1, 128), f32),
+            pltpu.VMEM((16, 1, 128), f32),
+            pltpu.VMEM((1, 128), f32),
+            pltpu.VMEM((32, 1, 128), f32),
             dma((BLOCKS // GROUP,)), dma((4,)), dma((4,)), dma((KINDS,)), dma((KINDS,)),
         ],
         compiler_params=pltpu.CompilerParams(

time: 40.3 us -> 38.7 us (0.960)
  Pallas kernels: 39.6 us -> 38 us
    pallas_call x1, Pallas kernels: 38.9 us -> 37.3 us  [shards(): pl.pallas_call(kernel, out_shape=(pltpu.VMEM((64, 64), f32), pltpu.VMEM((...]
where the time goes in v4:
time: 38.7 us; the launch traced here: 38.6 us
  Pallas kernels  38 us (98%)
  between operations  0.64 us (2%)
    pallas_call x1, Pallas kernels, shards(): pl.pallas_call(kernel, out_shape=(pltpu.VMEM((64, 64), f32), pltpu.VMEM((...  37.3 us

profile of v4, /device:TPU:1, one launch (start us, length us, event | category | flops | bytes accessed | tf_op | source)
XLA Modules:
  0.0 38.6 jit_solution(10733020021029142379)
XLA Ops:
  0.6 37.3 %cp_update.1 = (f32[64,64]{1,0:T(8,128)S(1)}, f32[64,64]{1,0:T(8,128)S(1)}) custom-call(bf16[2048,16,128]{2,1,0:T(8,128)(2,1)} %t_hbm.1, bf16[4,64]{1,0:T(4,128)(2,1)} %b_hbm.1, bf16[64,128]{1,0:T(8,128)(2,1)} %bitcast.1, f32[64,64]{1,0:T(8,128)} %a_hbm.1, s32[12]{0:T(128)} %restart_hbm.1), custom_call_target="tpu_custom_call" | custom-call | tf_op jit(solution)/shard_map/cp_update/pallas_call | solution.py:341
  37.9 0.6 %write_out.1 = (f32[64,64]{1,0:T(8,128)}, f32[64,64]{1,0:T(8,128)}) custom-call(f32[64,64]{1,0:T(8,128)S(1)} %get-tuple-element.4.up_ref, f32[64,64]{1,0:T(8,128)S(1)} %get-tuple-element.5.gram_ref), custom_call_target="tpu_custom_call" | custom-call | tf_op jit(solution)/shard_map/write_out/pallas_call | solution.py:382

commit v5 on v4

--- a/solution.py
+++ b/solution.py
@@ -15,6 +15,9 @@
 OFFSET = 32767
 STEPS = 2.0 * OFFSET
 B, C, B_ALL, CORE, PLANE, PLANE_STEP, Z, Z_STEP, XY, XY_STEP, KINDS = range(11)
+
+Z_ORDER = (9, 7, 11, 8, 5, 13, 6, 10, 3, 15, 4, 12, 1, 2, 14)
+XY_ORDER = (21, 13, 19, 23, 29, 20, 5, 11, 15, 17, 27, 31, 12, 18, 22, 28, 3, 7, 9, 25, 4, 10, 14, 16, 26, 30, 1, 2, 6, 8, 24)
 
 
 def far_first(n):
@@ -125,6 +128,14 @@
         prod[pl.ds(n * GROUP, GROUP)] = out.reshape(GROUP, HALF * 16, 128)
 
 
+    tval = jnp.ones((8, 128), f32)
+    for step in range(ITERS):
+        flag = flags[step].astype(f32)
+        tval = flag + (1.0 - flag) * tval
+        t_next = (1.0 + jnp.sqrt(1.0 + 4.0 * tval * tval)) / 2.0
+        coef[step] = (tval - 1.0) / t_next
+        tval = t_next
+
     pl.semaphore_wait(barrier, 63)
 
     def b_copy(n):
@@ -175,6 +186,15 @@
         block_sum(n, 1 - core, give)
         core_copy(n).start()
 
+    def ball_copy(n):
+        to = (ja + n) % 8
+        return remote(
+            b_all.at[ja], b_all.at[ja], sent.at[B_ALL], got_all.at[B_ALL], device((to // 2) * 2 + z_lo, x, y, to % 2)
+        )
+
+    for n in range(1, 8):
+        ball_copy(n).start()
+
     @pl.loop(0, 16)
     def _(n):
         block_sum(n, core, mine)
@@ -192,15 +212,6 @@
             out_rs[n], out_step[n] = encode(mine[n] + got[n])
             plane_copy(n, out_rs, in_rs, PLANE).start()
             plane_copy(n, out_step, in_step, PLANE_STEP).start()
-
-    def ball_copy(n):
-        to = (ja + n) % 8
-        return remote(
-            b_all.at[ja], b_all.at[ja], sent.at[B_ALL], got_all.at[B_ALL], device((to // 2) * 2 + z_lo, x, y, to % 2)
-        )
-
-    for n in range(1, 8):
-        ball_copy(n).start()
 
     exchange(ct_all.at[0:3], C).wait()
     exchange(b_all.at[0:7], B_ALL).wait()
@@ -219,23 +230,15 @@
     weight_g[...] = jnp.concatenate([both, both], 0)
     inverse = 1.0 / lip
 
-    tval = jnp.ones((8, 128), f32)
-    for step in range(ITERS):
-        flag = flags[step].astype(f32)
-        tval = flag + (1.0 - flag) * tval
-        t_next = (1.0 + jnp.sqrt(1.0 + 4.0 * tval * tval)) / 2.0
-        coef[step] = (tval - 1.0) / t_next
-        tval = t_next
-
-    start = a_in[...]
-    current = jnp.concatenate([start[:HALF], start[HALF:]], 1)
-
     total = mine[15] + got[15]
     exchange(in_step.at[0:15], PLANE_STEP).wait_recv()
     exchange(in_rs.at[0:15], PLANE).wait_recv()
     for n in range(15):
         total = total + decode(in_rs[n], in_step[n])
     target_term = total * inverse
+
+    start = a_in[...]
+    current = jnp.concatenate([start[:HALF], start[HALF:]], 1)
 
     look = current
     weights = weight_g[...]
@@ -263,8 +266,8 @@
     gram_out[1], gram_step[1] = encode(packed[16:])
 
     def z_peer(n):
-        step = (4, 3, 5, 2, 6, 1, 7, 0)[n // 2]
-        return (z + step) % 8, (core + n % 2) % 2
+        step, other = divmod(Z_ORDER[n], 2)
+        return (z + step) % 8, (core + other) % 2
 
     def z_copy(n, src, dst, kind):
         to_z, to_core = z_peer(n)
@@ -272,10 +275,9 @@
             src.at[to_core], dst.at[core * 8 + z], sent.at[kind], got_all.at[kind], device(to_z, x, y, to_core)
         )
 
-    for n in range(16):
-        if n != 14:
-            z_copy(n, gram_out, gram_z, Z).start()
-            z_copy(n, gram_step, gram_z_step, Z_STEP).start()
+    for n in range(15):
+        z_copy(n, gram_out, gram_z, Z).start()
+        z_copy(n, gram_step, gram_z_step, Z_STEP).start()
     gram_z[core * 8 + z] = gram_out[core]
     gram_z_step[core * 8 + z] = gram_step[core]
     up_ref[0:HALF, :] = current[:, :64]
@@ -288,17 +290,16 @@
     gram_half[...], half_step[...] = encode(half)
 
     def xy_copy(n, src, dst, kind):
-        step = (10, 11, 9, 14, 6, 8, 2, 15, 13, 7, 5, 12, 4, 3, 1, 0)[n // 2]
+        step, other = divmod(XY_ORDER[n], 2)
         to_x, to_y = (x + step // 4) % 4, (y + step % 4) % 4
-        to_core = (core + n % 2) % 2
+        to_core = (core + other) % 2
         return remote(
             src, dst.at[core * 16 + x * 4 + y], sent.at[kind], got_all.at[kind], device(z, to_x, to_y, to_core)
         )
 
-    for n in range(32):
-        if n != 30:
-            xy_copy(n, gram_half, gram_xy, XY).start()
-            xy_copy(n, half_step, gram_xy_step, XY_STEP).start()
+    for n in range(31):
+        xy_copy(n, gram_half, gram_xy, XY).start()
+        xy_copy(n, half_step, gram_xy_step, XY_STEP).start()
     gram_xy[core * 16 + x * 4 + y] = gram_half[...]
     gram_xy_step[core * 16 + x * 4 + y] = half_step[...]
     exchange(gram_xy.at[0:31], XY).wait_recv()

time: 38.7 us -> 37.9 us (0.979)
  Pallas kernels: 38 us -> 37.2 us
    pallas_call x1, Pallas kernels: 37.3 us -> 36.5 us  [shards(): pl.pallas_call(kernel, out_shape=(pltpu.VMEM((64, 64), f32), pltpu.VMEM((...]
where the time goes in v5:
time: 37.9 us; the launch traced here: 37.8 us
  Pallas kernels  37.2 us (98%)
  between operations  0.64 us (2%)
    pallas_call x1, Pallas kernels, shards(): pl.pallas_call(kernel, out_shape=(pltpu.VMEM((64, 64), f32), pltpu.VMEM((...  36.5 us

profile of v5, /device:TPU:1, one launch (start us, length us, event | category | flops | bytes accessed | tf_op | source)
XLA Modules:
  0.0 37.8 jit_solution(7675481722932644649)
XLA Ops:
  0.6 36.5 %cp_update.1 = (f32[64,64]{1,0:T(8,128)S(1)}, f32[64,64]{1,0:T(8,128)S(1)}) custom-call(bf16[2048,16,128]{2,1,0:T(8,128)(2,1)} %t_hbm.1, bf16[4,64]{1,0:T(4,128)(2,1)} %b_hbm.1, bf16[64,128]{1,0:T(8,128)(2,1)} %bitcast.1, f32[64,64]{1,0:T(8,128)} %a_hbm.1, s32[12]{0:T(128)} %restart_hbm.1), custom_call_target="tpu_custom_call" | custom-call | tf_op jit(solution)/shard_map/cp_update/pallas_call | solution.py:342
  37.2 0.6 %write_out.1 = (f32[64,64]{1,0:T(8,128)}, f32[64,64]{1,0:T(8,128)}) custom-call(f32[64,64]{1,0:T(8,128)S(1)} %get-tuple-element.4.up_ref, f32[64,64]{1,0:T(8,128)S(1)} %get-tuple-element.5.gram_ref), custom_call_target="tpu_custom_call" | custom-call | tf_op jit(solution)/shard_map/write_out/pallas_call | solution.py:383

commit v6 on v5

--- a/solution.py
+++ b/solution.py
@@ -95,9 +95,10 @@
     def greet(to):
         pl.semaphore_signal(barrier, inc=1, device_id=to, device_id_type=MESH)
 
-    @pl.loop(1, 32)
-    def _(n):
-        greet(device((z + 2 * (n // 8)) % 8, x, (y + (n // 2) % 4) % 4, (core + n % 2) % 2))
+    @pl.loop(0, 31)
+    def _(n):
+        to_z, to_y = (z + 2 * far_first(n // 8)) % 8, (y + far_first((n // 2) % 4)) % 4
+        greet(device(to_z, x, to_y, (core + 1 + n % 2) % 2))
 
     @pl.loop(0, 8)
     def _(n):
@@ -179,7 +180,7 @@
             out[n, group * 8 : group * 8 + 8, :] = add_rows(stack, row)
 
     def core_copy(n):
-        return remote(give.at[n], got.at[n], sent.at[CORE], core_r.at[n // 4], device(z, x, y, 1 - core))
+        return remote(give.at[n], got.at[n], sent.at[CORE], core_r.at[n // 2], device(z, x, y, 1 - core))
 
     @pl.loop(0, 16)
     def _(n):
@@ -203,13 +204,14 @@
         to_z, to_y = target(n)
         return remote(src.at[n], dst.at[n], sent.at[kind], got_all.at[kind], device(to_z * 2 + z_lo, x, to_y, core))
 
-    for part in range(4):
-        blocks = got.at[4 * part : 4 * part + 4]
+    for part in range(8):
+        blocks = got.at[2 * part : 2 * part + 2]
         remote(blocks, blocks, sent.at[CORE], core_r.at[part], device(z, x, y, 1 - core)).wait_recv()
 
-        @pl.loop(4 * part, min(4 * part + 4, 15))
-        def _(n):
+        group = range(2 * part, min(2 * part + 2, 15))
+        for n in group:
             out_rs[n], out_step[n] = encode(mine[n] + got[n])
+        for n in group:
             plane_copy(n, out_rs, in_rs, PLANE).start()
             plane_copy(n, out_step, in_step, PLANE_STEP).start()
 
@@ -373,7 +375,7 @@
             pltpu.VMEM((16, 1, 128), f32),
             pltpu.VMEM((1, 128), f32),
             pltpu.VMEM((32, 1, 128), f32),
-            dma((BLOCKS // GROUP,)), dma((4,)), dma((4,)), dma((KINDS,)), dma((KINDS,)),
+            dma((BLOCKS // GROUP,)), dma((4,)), dma((8,)), dma((KINDS,)), dma((KINDS,)),
         ],
         compiler_params=pltpu.CompilerParams(
             collective_id=0, has_side_effects=True, vmem_limit_bytes=32 * 2**20

time: 37.9 us -> 37.4 us (0.987)
  Pallas kernels: 37.2 us -> 36.7 us
    pallas_call x1, Pallas kernels: 36.5 us -> 36.1 us  [shards(): pl.pallas_call(kernel, out_shape=(pltpu.VMEM((64, 64), f32), pltpu.VMEM((...]
where the time goes in v6:
time: 37.4 us
  Pallas kernels  36.7 us (98%)
  between operations  0.64 us (2%)
    pallas_call x1, Pallas kernels, shards(): pl.pallas_call(kernel, out_shape=(pltpu.VMEM((64, 64), f32), pltpu.VMEM((...  36.1 us

profile of v6, /device:TPU:1, one launch (start us, length us, event | category | flops | bytes accessed | tf_op | source)
XLA Modules:
  0.0 37.4 jit_solution(16883675991325716293)
XLA Ops:
  0.6 36.1 %cp_update.1 = (f32[64,64]{1,0:T(8,128)S(1)}, f32[64,64]{1,0:T(8,128)S(1)}) custom-call(bf16[2048,16,128]{2,1,0:T(8,128)(2,1)} %t_hbm.1, bf16[4,64]{1,0:T(4,128)(2,1)} %b_hbm.1, bf16[64,128]{1,0:T(8,128)(2,1)} %bitcast.1, f32[64,64]{1,0:T(8,128)} %a_hbm.1, s32[12]{0:T(128)} %restart_hbm.1), custom_call_target="tpu_custom_call" | custom-call | tf_op jit(solution)/shard_map/cp_update/pallas_call | solution.py:344
  36.7 0.6 %write_out.1 = (f32[64,64]{1,0:T(8,128)}, f32[64,64]{1,0:T(8,128)}) custom-call(f32[64,64]{1,0:T(8,128)S(1)} %get-tuple-element.4.up_ref, f32[64,64]{1,0:T(8,128)S(1)} %get-tuple-element.5.gram_ref), custom_call_target="tpu_custom_call" | custom-call | tf_op jit(solution)/shard_map/write_out/pallas_call | solution.py:385
